TPU v7x, 32 devices: a whole 2x2x4 slice. The times are simulated.
32 devices in a mesh: groups: 2 (over x), frag: 16 (over z, y, core).
Axes of the slice: x: 2, y: 2, z: 4, core: 2. Of those that a mesh axis runs over, the one named last changes fastest.
Arguments:
- density: bfloat16 [64, 512, 512], P(('groups', 'frag')), parts along dimension 0, may hold values from -2 to 2
- hcore: bfloat16 [64, 512, 512], P(('groups', 'frag')), parts along dimension 0, may hold values from -6 to 6
- kernel: bfloat16 [64, 512, 512], P(('groups', 'frag')), parts along dimension 0, may hold values from -0.25 to 0.25
- coupling: bfloat16 [64, 4, 512, 512], P(('groups', 'frag')), parts along dimension 0, may hold values from -0.25 to 0.25
- partners: int32 [32, 4], replicated, may hold values from 0 to 31, as said below
- pair_count: int32 [32], replicated, may hold values from 1 to 4
- charge_map: bfloat16 [64, 512, 128], P(('groups', 'frag')), parts along dimension 0, may hold values from -0.25 to 0.25
- charge_pos: float32 [64, 3, 128], P(('groups', 'frag')), parts along dimension 0, may hold values from 0 to 4
- grid_pos: float32 [64, 3, 256], P(('groups', 'frag')), parts along dimension 0, may hold values from 0 to 4
- grid_basis: bfloat16 [64, 512, 256], P(('groups', 'frag')), parts along dimension 0, may hold values from -0.375 to 0.375
Outputs:
- fock: float32 [64, 512, 512], P(('groups', 'frag')), parts along dimension 0
There are 2 independent parts, one for each index of `groups`. A program takes and returns all parts, laid end to end along the dimension named above; an argument that names none is the same for every part. Nothing has to cross between parts.
Inputs may be any that keep to these rules, and one draw needn't show every extreme that they name: partners[I, k] is never I and lies on device I // 2 or on one of the two devices beside it, fragment F lying on device F // 2.
All inputs are finite; a program needn't handle non-finite values.
Results may differ from a plain program's by a relative error of at most 0.0028.
Values may be sent and summed in bfloat16 or wider, within the bound.
A program may use at most 192 MiB of HBM per device.

v0:
```python
import jax
import jax.numpy as jnp
from jax import lax
from jax.sharding import PartitionSpec as P


def extended(x, sides, width):
    for axis, dim in sides:
        peers, length = (lax.axis_size(axis), x.shape[dim])
        up = [(i, (i + 1) % peers) for i in range(peers - 1)]
        down = [(j, i) for i, j in up]
        last = lax.slice_in_dim(x, length - width, length, axis=dim)
        leading = lax.slice_in_dim(x, 0, width, axis=dim)
        before = lax.ppermute(last, axis, up)
        after = lax.ppermute(leading, axis, down)
        x = jnp.concatenate([before, x, after], axis=dim)
    return x


def shifted(value, axis, steps):
    count = lax.axis_size(axis)
    leading, last = (max(0, -steps), min(count, count - steps))
    return lax.ppermute(value, axis, [(source, source + steps) for source in range(leading, last)])


def potential_at(grid, owners, charges, places, sources):
    dist_sq = jnp.zeros(
        (grid.shape[0], grid.shape[2], places.shape[0], places.shape[2]), jnp.float32
    )
    for coord in range(3):
        delta = grid[:, coord, :, None, None] - places[None, None, :, coord, :]
        dist_sq = dist_sq + delta * delta
    weights = charges[None, None, :, :] / jnp.sqrt(dist_sq + 1.0)
    keep = owners[:, None] != sources[None, :]
    weights = jnp.where(keep[:, None, :, None], weights, 0.0)
    return jnp.sum(weights, axis=(2, 3))


def body(
    density,
    hcore,
    kernel,
    coupling,
    partners,
    pair_count,
    charge_map,
    charge_pos,
    grid_pos,
    grid_basis,
):
    local = density.shape[0]
    slots = coupling.shape[1]
    basis = density.shape[1]
    device = lax.axis_index("frag")
    first = device * local
    own_ids = first + jnp.arange(local, dtype=jnp.int32)
    own_partners = lax.dynamic_slice_in_dim(partners, first, local, 0)
    own_count = lax.dynamic_slice_in_dim(pair_count, first, local, 0)
    window = extended(density, (("frag", 0),), local)
    populations = jnp.diagonal(density, axis1=1, axis2=2).astype(jnp.float32)
    charges = jnp.einsum(
        "fm,fma->fa", populations, charge_map.astype(jnp.float32), precision=lax.Precision.HIGHEST
    )
    empty = jnp.zeros((local, grid_pos.shape[2]), jnp.float32)
    pieces = (
        lax.all_gather(charges, "frag", axis=0, tiled=True),
        lax.all_gather(charge_pos, "frag", axis=0, tiled=True),
    )
    sources = jnp.arange(pieces[0].shape[0], dtype=jnp.int32)
    field = empty + potential_at(grid_pos, own_ids, pieces[0], pieces[1], sources)
    scaled = (grid_basis.astype(jnp.float32) * field[:, None, :]).astype(jnp.bfloat16)
    embed = jnp.einsum("fmg,fng->fmn", scaled, grid_basis, preferred_element_type=jnp.float32)
    monomer = jnp.einsum("fmn,fnp->fmp", density, kernel, preferred_element_type=jnp.float32)
    half_step = jnp.einsum(
        "fmn,fknp->fkmp", density, coupling, preferred_element_type=jnp.float32
    ).astype(jnp.bfloat16)
    position = own_partners - (device - 1) * local
    partner_dens = jnp.take(window, position.reshape(-1), axis=0).reshape(
        local, slots, basis, basis
    )
    dimer = jnp.einsum(
        "fkmn,fknp->fkmp", half_step, partner_dens, preferred_element_type=jnp.float32
    )
    live = (jnp.arange(slots, dtype=jnp.int32)[None, :] < own_count[:, None]).astype(jnp.float32)
    own_sum = jnp.einsum("fk,fkmp->fmp", live, dimer, precision=lax.Precision.HIGHEST)
    targets = (
        position[:, :, None] == jnp.arange(3 * local, dtype=jnp.int32)[None, None, :]
    ).astype(jnp.float32) * live[:, :, None]
    returned = jnp.einsum("fkw,fkmp->wpm", targets, dimer, precision=lax.Precision.HIGHEST)
    to_lower = returned[:local]
    to_upper = returned[2 * local :]
    arrived = jnp.zeros((local, basis, basis), jnp.float32)
    for offset, outgoing in ((1, to_upper), (-1, to_lower)):
        arrived = arrived + shifted(outgoing, "frag", offset)
    return (
        hcore.astype(jnp.float32)
        + monomer
        + embed
        + own_sum
        + returned[local : 2 * local]
        + arrived
    )


def solution(mesh):
    in_specs = (
        P(("groups", "frag"), None, None),
        P(("groups", "frag"), None, None),
        P(("groups", "frag"), None, None),
        P(("groups", "frag"), None, None, None),
        P(),
        P(),
        P(("groups", "frag"), None, None),
        P(("groups", "frag"), None, None),
        P(("groups", "frag"), None, None),
        P(("groups", "frag"), None, None),
    )
    out_specs = P(("groups", "frag"), None, None)
    return jax.shard_map(body, mesh=mesh, in_specs=in_specs, out_specs=out_specs, check_vma=False)
```

profile of v0, /device:TPU:1, one launch (start us, length us, event | category | flops | bytes accessed | tf_op | source)
XLA Modules:
  0.0 221.6 jit_solution(7397415609076141947)
XLA Ops:
  0.0 4.7 %collective-permute-start = (bf16[2,512,512]{2,1,0:T(8,128)(2,1)}, bf16[2,512,512]{2,1,0:T(8,128)(2,1)S(1)}, u32[]{:S(2)}, u32[]{:S(2)}) collective-permute-start(bf16[2,512,512]{2,1,0:T(8,128)(2,1)} %param.10), channel_id=1, source_target_pairs={{0,1},{1,2},{2,3},{3,4},{4,5},{5,6},{6,7},{7,8},{8,9},{9,10},{10,1... | collective-permute-start | bytes 3145736 | tf_op jit(solution)/shard_map/ppermute | solution.py:14
  4.7 1.9 collective-permute-start.1
  6.6 0.8 compare_and_fusion
  7.6 0.6 fusion.26
  8.7 42.4 %copy.32 = bf16[2,512,512]{0,2,1:T(8,128)(2,1)} copy(bf16[2,512,512]{2,1,0:T(8,128)(2,1)} %param.10) | data formatting | bytes 2097152 | tf_op args[0]
  51.1 0.7 copy.35
  52.4 6.5 %gather_fusion = bf16[512,2]{1,0:T(8,128)(2,1)S(1)} fusion(bf16[2,512,512]{0,2,1:T(8,128)(2,1)} %copy.32, s32[512]{0:T(512)S(1)} %bitcast.45), kind=kCustom, calls=%fused_computation | custom fusion | bytes 8192 | tf_op jit(solution)/shard_map/jit(diagonal)/gather | solution.py:60
  59.0 22.2 %all_gather.7 = f32[32,3,128]{2,1,0:T(4,128)S(1)} all-gather(f32[2,3,128]{2,1,0:T(4,128)S(1)} %copy.33), channel_id=1, replica_groups=mesh['groups'=2,'frag'=16] {'frag'}, dimensions={0}, use_global_device_ids=true | all-gather | bytes 52224 | tf_op jit(solution)/shard_map/all_gather | solution.py:67
  81.2 0.7 pad_clamp_fusion
  81.9 0.7 fusion.25
  82.6 0.7 iota_compare_fusion.3
  83.4 2.9 %pad_maximum_fusion = bf16[6,512,512]{2,1,0:T(8,128)(2,1)} fusion(bf16[2,512,512]{2,1,0:T(8,128)(2,1)} %collective-permute-done.1, bf16[2,512,512]{2,1,0:T(8,128)(2,1)S(1)} %copy-done.1, bf16[2,512,512]{2,1,0:T(8,128)(2,1)S(1)} %collective-permute-done), kind=kLoop, calls=%fused_computation.12 | loop fusion | flops 3145728 | bytes 6291456 | tf_op jit(solution)/shard_map/concatenate | solution.py:16
  86.3 4.7 %gather_fusion.1 = bf16[8,512,512]{2,1,0:T(8,128)(2,1)} fusion(bf16[6,512,512]{2,1,0:T(8,128)(2,1)} %pad_maximum_fusion, s32[1024]{0:T(1024)S(1)} %pad_clamp_fusion), kind=kCustom, calls=%fused_computation.1 | custom fusion | bytes 8388640 | tf_op jit(solution)/shard_map/jit(_take)/gather | solution.py:78
  91.0 12.0 %fusion.4 = f32[2,4,512,512]{3,2,1,0:T(8,128)} fusion(bf16[2,4,512,512]{3,2,1,0:T(8,128)(2,1)} %bitcast.50, pred[2,4]{1,0:T(4,128)(4,1)S(1)} %copy-done.10, bf16[2,4,512,512]{3,2,1,0:T(8,128)(2,1)} %param.13, bf16[2,512,512]{2,1,0:T(8,128)(2,1)S(1)} %copy-done.1), kind=kOutput, calls=%fused_computation.7 | convolution fusion | flops 4299161600 | bytes 17825800 | tf_op jit(solution)/shard_map/fkmn,fknp->fkmp/dot_general | solution.py:81
  103.0 23.4 %fusion.8 = f32[512,512,6]{1,2,0:T(8,128)} fusion(f32[2,4,512,512]{3,2,1,0:T(8,128)} %fusion.4, f32[2,4]{1,0:T(2,128)S(1)} %get-tuple-element.16, s32[2,4]{1,0:T(2,128)S(1)} %copy-done.7), kind=kOutput, calls=%fused_computation.11 | convolution fusion | flops 150995040 | bytes 14680128 | tf_op jit(solution)/shard_map/fkw,fkmp->wpm/dot_general | solution.py:89
  126.5 9.1 %copy.40 = f32[512,512,6]{0,1,2:T(8,128)} copy(f32[512,512,6]{1,2,0:T(8,128)} %fusion.8) | data formatting | bytes 12582912 | tf_op jit(solution)/shard_map/fkw,fkmp->wpm/dot_general | solution.py:89
  135.6 2.8 %fusion.29 = (f32[2,512,512]{2,1,0:T(8,128)S(1)}, f32[2,512,512]{2,1,0:T(8,128)S(1)}) fusion(f32[6,512,512]{2,1,0:T(8,128)} %bitcast.48), kind=kLoop, calls=%fused_computation.45 | loop fusion | bytes 8388608 | tf_op jit(solution)/shard_map/slice | solution.py:90
  138.4 2.2 collective-permute-start.2
  140.6 2.5 %collective-permute-start.3 = (f32[2,512,512]{2,1,0:T(8,128)S(1)}, f32[2,512,512]{2,1,0:T(8,128)S(1)}, u32[]{:S(2)}, u32[]{:S(2)}) collective-permute-start(f32[2,512,512]{2,1,0:T(8,128)S(1)} %get-tuple-element.7), channel_id=1, source_target_pairs={{1,0},{2,1},{3,2},{4,3},{5,4},{6,5},{7,6},{8,7},{9,8},{10,9},{11,1... | collective-permute-start | bytes 6291464 | tf_op jit(solution)/shard_map/ppermute | solution.py:23
  143.2 53.0 %all-gather = f32[16,2,128]{2,1,0:T(2,128)S(1)} all-gather(f32[1,2,128]{2,1,0:T(2,128)S(1)} %bitcast.56), channel_id=1, replica_groups=mesh['groups'=2,'frag'=16] {'frag'}, dimensions={0}, use_global_device_ids=true | all-gather | bytes 17408 | tf_op jit(solution)/shard_map/all_gather | solution.py:66
  196.2 0.7 fusion.31
  196.9 9.1 %select_reduce_fusion = f32[2,256]{1,0:T(2,128)S(1)} fusion(f32[32,128]{1,0:T(8,128)S(1)} %bitcast.54, f32[2,256]{1,0:T(2,128)S(1)} %get-tuple-element.13, f32[32,128]{1,0:T(8,128)S(1)} %bitcast.55, f32[2,256]{1,0:T(2,128)S(1)} %get-tuple-element.14, f32[32,128]{1,0:T(8,128)S(1)} %bitcast.53, f32[2,256]{1,0:T(2,128)S(1)} %get-tuple-element.12, ...), kind=kLoop, calls=%fused_computation.6 | loop fusion | flops 25165312 | bytes 73792 | tf_op jit(solution)/shard_map/reduce_sum | solution.py:36
  206.1 11.6 %fusion = f32[2,1,512,512]{3,1,2,0:T(1,128)S(1)} fusion(f32[2,4,512,512]{3,2,1,0:T(8,128)S(1)} %bitcast.47, pred[2,4,1,1]{1,0,2,3:T(4,128)(4,1)S(1)} %get-tuple-element.15), kind=kOutput, calls=%fused_computation.2 | convolution fusion | flops 25165824 | bytes 10485768 | tf_op jit(solution)/shard_map/fk,fkmp->fmp/dot_general | solution.py:85
  217.7 3.8 %fusion.13 = f32[2,512,512]{2,1,0:T(8,128)} fusion(f32[6,512,512]{2,1,0:T(8,128)} %bitcast.49, f32[2,1,512,512]{3,1,2,0:T(1,128)S(1)} %fusion, f32[2,512,512]{2,1,0:T(8,128)S(1)} %collective-permute-done.2, f32[2,512,512]{2,1,0:T(8,128)S(1)} %collective-permute-done.3, f32[2,512,512]{2,1,0:T(8,128)S(1)} %fusion.31, bf16[2,512,512]{2,1,0:T(8,128)(2,1)S(1)} %copy-done.3, ...), kind=kOutput, calls=%fused_computation.15 | convolution fusion | flops 272891904 | bytes 14682112 | tf_op jit(solution)/shard_map/fmg,fng->fmn/dot_general | solution.py:72
  (41 shorter events, 1.7 us)
Async XLA Ops:
  0.0 196.2 %copy-start = (bf16[2,512,512]{2,1,0:T(8,128)(2,1)S(1)}, bf16[2,512,512]{2,1,0:T(8,128)(2,1)}, u32[]{:S(2)}) copy-start(bf16[2,512,512]{2,1,0:T(8,128)(2,1)} %param.12) | copy-start | bytes 3145732
  0.0 83.4 %collective-permute-start = (bf16[2,512,512]{2,1,0:T(8,128)(2,1)}, bf16[2,512,512]{2,1,0:T(8,128)(2,1)S(1)}, u32[]{:S(2)}, u32[]{:S(2)}) collective-permute-start(bf16[2,512,512]{2,1,0:T(8,128)(2,1)} %param.10), channel_id=1, source_target_pairs={{0,1},{1,2},{2,3},{3,4},{4,5},{5,6},{6,7},{7,8},{8,9},{9,10},{10,1... | collective-permute-start | bytes 3145736 | tf_op jit(solution)/shard_map/ppermute | solution.py:14
  4.7 78.8 %collective-permute-start.1 = (bf16[2,512,512]{2,1,0:T(8,128)(2,1)}, bf16[2,512,512]{2,1,0:T(8,128)(2,1)}, u32[]{:S(2)}, u32[]{:S(2)}) collective-permute-start(bf16[2,512,512]{2,1,0:T(8,128)(2,1)} %param.10), channel_id=1, source_target_pairs={{1,0},{2,1},{3,2},{4,3},{5,4},{6,5},{7,6},{8,7},{9,8},{10,9},{11,1... | collective-permute-start | bytes 3145736 | tf_op jit(solution)/shard_map/ppermute | solution.py:15
  7.5 0.7 copy-start.6
  8.7 43.1 %copy-start.9 = (s32[32]{0:T(128)S(1)}, s32[32]{0:T(128)}, u32[]{:S(2)}) copy-start(s32[32]{0:T(128)} %param.15) | copy-start | bytes 388
  8.7 43.7 %copy-start.8 = (f32[2,3,128]{2,0,1:T(2,128)S(1)}, f32[2,3,128]{2,0,1:T(2,128)}, u32[]{:S(2)}) copy-start(f32[2,3,128]{2,0,1:T(2,128)} %param.17) | copy-start | bytes 9220
  8.7 74.6 %copy-start.5 = (f32[2,3,256]{2,0,1:T(2,128)S(1)}, f32[2,3,256]{2,0,1:T(2,128)}, u32[]{:S(2)}) copy-start(f32[2,3,256]{2,0,1:T(2,128)} %param.18) | copy-start | bytes 18436
  8.7 74.6 %copy-start.4 = (bf16[2,512,128]{2,1,0:T(8,128)(2,1)S(1)}, bf16[2,512,128]{2,1,0:T(8,128)(2,1)}, u32[]{:S(2)}) copy-start(bf16[2,512,128]{2,1,0:T(8,128)(2,1)} %param.16) | copy-start | bytes 786436
  8.7 74.7 %copy-start.1 = (bf16[2,512,512]{2,1,0:T(8,128)(2,1)S(1)}, bf16[2,512,512]{2,1,0:T(8,128)(2,1)}, u32[]{:S(2)}) copy-start(bf16[2,512,512]{2,1,0:T(8,128)(2,1)} %param.10) | copy-start | bytes 3145732
  86.3 4.7 %copy-start.10 = (pred[2,4]{1,0:T(4,128)(4,1)S(1)}, pred[2,4]{1,0:T(4,128)(4,1)}, u32[]{:S(2)}) copy-start(pred[2,4]{1,0:T(4,128)(4,1)} %copy.35) | copy-start | bytes 28
  91.0 12.0 %copy-start.7 = (s32[2,4]{1,0:T(2,128)S(1)}, s32[2,4]{1,0:T(2,128)}, u32[]{:S(2)}) copy-start(s32[2,4]{1,0:T(2,128)} %copy-done.6) | copy-start | bytes 100
  135.6 70.5 %slice-start = ((s8[8388608]{0:T(1024)(128)(4,1)}), s8[4194304]{0:T(1024)(128)(4,1)S(1)}, s32[]{:S(2)}) async-start(s8[8388608]{0:T(1024)(128)(4,1)} %bitcast.46), calls=%async_computation | async-start | bytes 8388608
  135.6 70.5 %slice-start.1 = ((s8[8388608]{0:T(1024)(128)(4,1)}), s8[4194304]{0:T(1024)(128)(4,1)S(1)}, s32[]{:S(2)}) async-start(s8[8388608]{0:T(1024)(128)(4,1)} %bitcast.46), calls=%async_computation.1 | async-start | bytes 8388608
  138.4 79.3 %collective-permute-start.2 = (f32[2,512,512]{2,1,0:T(8,128)S(1)}, f32[2,512,512]{2,1,0:T(8,128)S(1)}, u32[]{:S(2)}, u32[]{:S(2)}) collective-permute-start(f32[2,512,512]{2,1,0:T(8,128)S(1)} %get-tuple-element.8), channel_id=1, source_target_pairs={{0,1},{1,2},{2,3},{3,4},{4,5},{5,6},{6,7},{7,8},{8,9},{9,10},{10,1... | collective-permute-start | bytes 6291464 | tf_op jit(solution)/shard_map/ppermute | solution.py:23
  140.6 77.1 %collective-permute-start.3 = (f32[2,512,512]{2,1,0:T(8,128)S(1)}, f32[2,512,512]{2,1,0:T(8,128)S(1)}, u32[]{:S(2)}, u32[]{:S(2)}) collective-permute-start(f32[2,512,512]{2,1,0:T(8,128)S(1)} %get-tuple-element.7), channel_id=1, source_target_pairs={{1,0},{2,1},{3,2},{4,3},{5,4},{6,5},{7,6},{8,7},{9,8},{10,9},{11,1... | collective-permute-start | bytes 6291464 | tf_op jit(solution)/shard_map/ppermute | solution.py:23
  206.1 11.7 %copy-start.2 = (bf16[2,512,256]{2,1,0:T(8,128)(2,1)S(1)}, bf16[2,512,256]{2,1,0:T(8,128)(2,1)}, u32[]{:S(2)}) copy-start(bf16[2,512,256]{2,1,0:T(8,128)(2,1)} %param.19) | copy-start | bytes 1572868
  206.1 11.6 %copy-start.3 = (bf16[2,512,512]{2,1,0:T(8,128)(2,1)S(1)}, bf16[2,512,512]{2,1,0:T(8,128)(2,1)}, u32[]{:S(2)}) copy-start(bf16[2,512,512]{2,1,0:T(8,128)(2,1)} %param.11) | copy-start | bytes 3145732
where the time goes:
time: 225 us; the launch traced here: 222 us
  blocking collectives  75.3 us (33%)
  local copies, waits for them, and re-layouts  67.1 us (30%)
  matrix products  51.8 us (23%)
  other arithmetic  15.9 us (7%)
  starting transfers between devices  11.3 us (5%)
    all_gather x1, blocking collectives, body(): lax.all_gather(charges, 'frag', axis=0, tiled=True)  53 us
    unnamed x28, local copies, waits for them, and re-layouts  42.4 us
    dot_general x1, matrix products, body(): jnp.einsum('fkw,fkmp->wpm', targets, dimer, precision=lax.Precision.HIGHEST)  23.4 us
    all_gather x1, blocking collectives, body(): lax.all_gather(charge_pos, 'frag', axis=0, tiled=True)  22.2 us
    dot_general x1, matrix products, body(): jnp.einsum('fkmn,fknp->fkmp', half_step, partner_dens, preferred_element_...  12 us
    dot_general x1, matrix products, body(): jnp.einsum('fk,fkmp->fmp', live, dimer, precision=lax.Precision.HIGHEST)  11.6 us
    reduce_sum x1, other arithmetic, potential_at(): return jnp.sum(weights, axis=(2, 3))  9.11 us
    dot_general x1, local copies, waits for them, and re-layouts, body(): jnp.einsum('fkw,fkmp->wpm', targets, dimer, precision=lax.Precision.HIGHEST)  9.11 us
  transfers between devices with their start and end apart: 4, of which 0 were waited for; matrix products, arithmetic and copies ran while one was open for 34% of the time, Pallas kernels for 0%

commit v1 on v0

v1 whole, which is shorter than its diff:
```python
import functools

import jax
import jax.numpy as jnp
from jax import lax
from jax.experimental import pallas as pl
from jax.experimental.pallas import tpu as pltpu
from jax.sharding import PartitionSpec as P

MESH = pl.DeviceIdType.MESH
F32 = jnp.float32
BF16 = jnp.bfloat16


def dot(a, b):
    return jnp.dot(a, b, preferred_element_type=F32)


def dot_t(a, b):
    return lax.dot_general(a, b, (((1,), (1,)), ((), ())), preferred_element_type=F32)


def fock_kernel(
    n, rows,
    partners, pair_count, density, hcore, kernel, coupling, charge_map, charge_pos, grid_pos, grid_basis,
    fock,
    win, coup, resp, core, cmap, gbas, half, t_send, t_recv, t_own, dens_t, acc, pub, every, place,
    in_sem, out_sem, d_send_sem, d_recv_sem, t_send_sem, t_recv_sem, q_send_sem, q_recv_sem,
):
    local, basis = density.shape[0], density.shape[1]
    slots = coupling.shape[1]
    points = grid_pos.shape[2]
    pieces = basis // rows
    group = lax.axis_index("groups")
    me = lax.axis_index("frag")
    first = me * local
    has_low, has_up = me > 0, me < n - 1

    loads = [
        pltpu.make_async_copy(density, win.at[pl.ds(local, local)], in_sem.at[0]),
        pltpu.make_async_copy(charge_map, cmap, in_sem.at[1]),
        pltpu.make_async_copy(coupling, coup, in_sem.at[2]),
        pltpu.make_async_copy(kernel, resp, in_sem.at[3]),
        pltpu.make_async_copy(hcore, core, in_sem.at[4]),
        pltpu.make_async_copy(grid_basis, gbas, in_sem.at[5]),
    ]
    for load in loads:
        load.start()

    barrier = pltpu.get_barrier_semaphore()

    def greet(step, carry):
        pl.semaphore_signal(
            barrier, inc=1, device_id=(group, lax.rem(me + step, n)), device_id_type=MESH
        )
        return carry

    lax.fori_loop(1, n, greet, 0)
    pl.semaphore_wait(barrier, n - 1)

    def dens_copy(side, f):
        return pltpu.make_async_remote_copy(
            src_ref=density.at[f],
            dst_ref=win.at[f if side == 0 else 2 * local + f],
            send_sem=d_send_sem.at[side, f],
            recv_sem=d_recv_sem.at[side, f],
            device_id=(group, me + 1 if side == 0 else me - 1),
            device_id_type=MESH,
        )

    def term_copy(side, f, c):
        part = pl.ds(pl.multiple_of(c * rows, rows), rows)
        return pltpu.make_async_remote_copy(
            src_ref=t_send.at[side, f, part],
            dst_ref=t_recv.at[side, f, part],
            send_sem=t_send_sem.at[side, f, c],
            recv_sem=t_recv_sem.at[side, f, c],
            device_id=(group, me + 1 if side == 0 else me - 1),
            device_id_type=MESH,
        )

    sends_to = (has_up, has_low)
    gets_from = (has_low, has_up)
    for side in range(2):
        @pl.when(sends_to[side])
        def _():
            for f in range(local):
                dens_copy(side, f).start()

    loads[0].wait()
    loads[1].wait()
    edge = 128
    eye = lax.broadcasted_iota(jnp.int32, (edge, edge), 0) == lax.broadcasted_iota(
        jnp.int32, (edge, edge), 1
    )
    for f in range(local):
        total = jnp.zeros((1, cmap.shape[2]), F32)
        for b in range(basis // edge):
            span = pl.ds(b * edge, edge)
            block = win[local + f, span, span].astype(F32)
            pops = jnp.sum(jnp.where(eye, block, 0.0), axis=1, keepdims=True)
            total = total + jnp.sum(pops * cmap[f, span, :].astype(F32), axis=0, keepdims=True)
        pub[f, 0:1, :] = total
        pub[f, 1:4, :] = charge_pos[f]
    every[me] = pub[...]

    def publish(step):
        target = lax.rem(me + step, n)
        return pltpu.make_async_remote_copy(
            src_ref=pub,
            dst_ref=every.at[me],
            send_sem=q_send_sem.at[step],
            recv_sem=q_recv_sem.at[step],
            device_id=(group, target),
            device_id_type=MESH,
        )

    def publish_start(step, carry):
        publish(step).start()
        return carry

    lax.fori_loop(1, n, publish_start, 0)

    loads[2].wait()
    live, position = [], []
    for f in range(local):
        count = pair_count[first + f]
        for k in range(slots):
            live.append(jnp.where(k < count, 1.0, 0.0).astype(F32))
            position.append(partners[first + f, k] - (me - 1) * local)
    for f in range(local):
        for k in range(slots):
            half[f * slots + k] = (
                dot(win[local + f], coup[f, k]) * live[f * slots + k]
            ).astype(BF16)

    weights = [
        [jnp.where(p == w, 1.0, 0.0).astype(F32) for p in position] for w in range(3 * local)
    ]

    def gather_terms(step, carry):
        span = pl.ds(pl.multiple_of(step * 32, 32), 32)
        for c in range(basis // 128):
            cols = pl.ds(c * 128, 128)
            pieces_here = [half[i, span, cols].astype(F32) for i in range(local * slots)]
            for w in range(3 * local):
                value = pieces_here[0] * weights[w][0]
                for i in range(1, local * slots):
                    value = value + pieces_here[i] * weights[w][i]
                value = value.astype(BF16)
                if w < local:
                    t_send[1, w, span, cols] = value
                elif w < 2 * local:
                    t_own[w - local, span, cols] = value
                else:
                    t_send[0, w - 2 * local, span, cols] = value
        return carry

    per_piece = rows // 32
    for c in range(pieces):
        lax.fori_loop(c * per_piece, (c + 1) * per_piece, gather_terms, 0)
        for side in range(2):
            @pl.when(sends_to[side])
            def _():
                for f in range(local):
                    term_copy(side, f, c).start()

    loads[3].wait()
    loads[4].wait()
    for f in range(local):
        own = win[local + f]
        dens_t[f] = own.T
        acc[f] = core[f].astype(F32) + dot(own, resp[f])
        acc[f] += dot_t(dens_t[f], t_own[f])

    def publish_wait(step, carry):
        publish(step).wait()
        return carry

    lax.fori_loop(1, n, publish_wait, 0)
    loads[5].wait()
    for f in range(local):
        for axis in range(3):
            place[axis] = jnp.broadcast_to(grid_pos[f, axis : axis + 1, :], (128, points)).T

        field_parts = []
        strip = 64
        for g in range(points // strip):
            span = pl.ds(g * strip, strip)
            px, py, pz = (place[axis, span, :] for axis in range(3))

            def add_source(source, total):
                for other in range(local):
                    keep = jnp.where(source * local + other == first + f, 0.0, 1.0).astype(F32)
                    rowsof = every[source, other]
                    dx = px - rowsof[1:2]
                    dy = py - rowsof[2:3]
                    dz = pz - rowsof[3:4]
                    total = total + (rowsof[0:1] * keep) * lax.rsqrt(
                        dx * dx + dy * dy + dz * dz + 1.0
                    )
                return total

            field_parts.append(lax.fori_loop(0, n, add_source, jnp.zeros((strip, 128), F32)))
        total = jnp.concatenate(field_parts, axis=0)
        field = jnp.sum(total.T, axis=0, keepdims=True)
        scaled = (gbas[f].astype(F32) * field).astype(BF16)
        acc[f] += dot_t(scaled, gbas[f])

    for side in range(2):
        @pl.when(gets_from[side])
        def _():
            for f in range(local):
                dens_copy(side, f).wait_recv()
    for f in range(local):
        for k in range(slots):
            where = jnp.clip(position[f * slots + k], 0, 3 * local - 1)
            acc[f] += dot(half[f * slots + k], win[where])

    for f in range(local):
        def add_piece(c, carry):
            part = pl.ds(pl.multiple_of(c * rows, rows), rows)
            for side in range(2):
                @pl.when(gets_from[side])
                def _():
                    term_copy(side, f, c).wait_recv()
                    acc[f, :, part] += dot_t(dens_t[f], t_recv[side, f, part, :])
            return carry

        lax.fori_loop(0, pieces, add_piece, 0)
        pltpu.make_async_copy(acc.at[f], fock.at[f], out_sem.at[f]).start()

    for side in range(2):
        @pl.when(sends_to[side])
        def _():
            for f in range(local):
                dens_copy(side, f).wait_send()
                for c in range(pieces):
                    term_copy(side, f, c).wait_send()
    for f in range(local):
        pltpu.make_async_copy(acc.at[f], fock.at[f], out_sem.at[f]).wait()


def body(
    density, hcore, kernel, coupling, partners, pair_count, charge_map, charge_pos, grid_pos, grid_basis
):
    n = lax.axis_size("frag")
    local, basis, _ = density.shape
    slots = coupling.shape[1]
    points = grid_pos.shape[2]
    charges = charge_map.shape[2]
    rows = 128
    pieces = basis // rows
    anywhere = pl.BlockSpec(memory_space=pl.ANY)
    smem = pl.BlockSpec(memory_space=pltpu.SMEM)
    vmem = pl.BlockSpec(memory_space=pltpu.VMEM)
    square = (basis, basis)
    dma = pltpu.SemaphoreType.DMA
    return pl.pallas_call(
        functools.partial(fock_kernel, n, rows),
        out_shape=jax.ShapeDtypeStruct((local,) + square, F32),
        in_specs=[smem, smem, anywhere, anywhere, anywhere, anywhere, anywhere, vmem, vmem, anywhere],
        out_specs=anywhere,
        scratch_shapes=[
            pltpu.VMEM((3 * local,) + square, BF16),
            pltpu.VMEM((local, slots) + square, BF16),
            pltpu.VMEM((local,) + square, BF16),
            pltpu.VMEM((local,) + square, BF16),
            pltpu.VMEM((local, basis, charges), BF16),
            pltpu.VMEM((local, basis, points), BF16),
            pltpu.VMEM((local * slots,) + square, BF16),
            pltpu.VMEM((2, local) + square, BF16),
            pltpu.VMEM((2, local) + square, BF16),
            pltpu.VMEM((local,) + square, BF16),
            pltpu.VMEM((local,) + square, BF16),
            pltpu.VMEM((local,) + square, F32),
            pltpu.VMEM((local, 4, charges), F32),
            pltpu.VMEM((n, local, 4, charges), F32),
            pltpu.VMEM((3, points, 128), F32),
            dma((6,)),
            dma((local,)),
            dma((2, local)),
            dma((2, local)),
            dma((2, local, pieces)),
            dma((2, local, pieces)),
            dma((n,)),
            dma((n,)),
        ],
        compiler_params=pltpu.CompilerParams(
            collective_id=0, has_side_effects=True, vmem_limit_bytes=48 * 1024 * 1024
        ),
    )(partners, pair_count, density, hcore, kernel, coupling, charge_map, charge_pos, grid_pos, grid_basis)


def solution(mesh):
    split = ("groups", "frag")
    block = P(split, None, None)
    in_specs = (
        block, block, block, P(split, None, None, None), P(), P(), block, block, block, block,
    )
    return jax.shard_map(body, mesh=mesh, in_specs=in_specs, out_specs=block, check_vma=False)
```

time: 225 us -> 65.5 us (0.29); the launches traced: 222 us -> 64.8 us
  blocking collectives: 75.3 us -> 0 us
  local copies, waits for them, and re-layouts: 67.1 us -> 9.78 us
  Pallas kernels: 0 us -> 55 us
  matrix products: 51.8 us -> 0 us
  other arithmetic: 15.9 us -> 0 us
  starting transfers between devices: 11.3 us -> 0 us
    all_gather x2 -> x0, blocking collectives: 75.3 us -> none  [the longest x1 53 us: body(): lax.all_gather(charges, 'frag', axis=0, tiled=True)]
    pallas_call x0 -> x1, Pallas kernels: none -> 55 us  [body(): pl.pallas_call(functools.partial(fock_kernel, n, rows), out_shape=jax.Sha...]
    dot_general x6 -> x0, matrix products: 51.8 us -> none  [the longest x1 23.4 us: body(): jnp.einsum('fkw,fkmp->wpm', targets, dimer, precision=lax.Precision.HIGHEST)]
    unnamed x28 -> x16, local copies, waits for them, and re-layouts: 42.4 us -> 9.78 us
    ppermute x4 -> x0, starting transfers between devices: 11.3 us -> none  [the longest x2 4.72 us: shifted(): lax.ppermute(value, axis, [(source, source + steps) for source in range(l...]
    gather x3 -> x0, local copies, waits for them, and re-layouts: 11.3 us -> none  [the longest x2 6.6 us: body(): populations = jnp.diagonal(density, axis1=1, axis2=2).astype(jnp.float32)]
    reduce_sum x1 -> x0, other arithmetic: 9.11 us -> none  [potential_at(): return jnp.sum(weights, axis=(2, 3))]
    dot_general x1 -> x0, local copies, waits for them, and re-layouts: 9.11 us -> none  [body(): jnp.einsum('fkw,fkmp->wpm', targets, dimer, precision=lax.Precision.HIGHEST)]
  transfers between devices with their start and end apart: 4 -> 0, of which waited for: 0 -> 0; matrix products, arithmetic and copies ran while one was open for 34% -> 0% of each run, Pallas kernels for 0% -> 0%
where the time goes in v1:
time: 65.5 us; the launch traced here: 64.8 us
  Pallas kernels  55 us (84%)
  local copies, waits for them, and re-layouts  9.78 us (15%)
    pallas_call x1, Pallas kernels, body(): pl.pallas_call(functools.partial(fock_kernel, n, rows), out_shape=jax.Sha...  55 us
    unnamed x16, local copies, waits for them, and re-layouts  9.78 us

profile of v1, /device:TPU:1, one launch (start us, length us, event | category | flops | bytes accessed | tf_op | source)
XLA Modules:
  0.0 64.8 jit_solution(4995256790020060556)
XLA Ops:
  0.0 0.7 %copy.12.charge_pos = f32[2,3,128]{2,1,0:T(4,128)S(1)} copy(f32[2,3,128]{2,0,1:T(2,128)} %param.17) | data formatting | bytes 6144 | tf_op args[7]
  0.7 0.7 %copy.13.grid_pos = f32[2,3,256]{2,1,0:T(4,128)S(1)} copy(f32[2,3,256]{2,0,1:T(2,128)} %param.18) | data formatting | bytes 12288 | tf_op args[8]
  1.4 0.8 %copy.11.partners = s32[32,4]{1,0:T(8,128)S(1)} copy(s32[32,4]{0,1:T(4,128)} %param.14) | data formatting | bytes 1024 | tf_op args[4]
  2.1 0.0 copy-start
  2.1 1.2 %copy-done = bf16[2,512,512]{2,1,0:T(8,128)(2,1)S(1)} copy-done((bf16[2,512,512]{2,1,0:T(8,128)(2,1)S(1)}, bf16[2,512,512]{2,1,0:T(8,128)(2,1)}, u32[]{:S(2)}) %copy-start) | copy-done | bytes 1048600
  3.4 0.0 copy-start.1
  3.4 1.2 %copy-done.1 = bf16[2,512,512]{2,1,0:T(8,128)(2,1)S(1)} copy-done((bf16[2,512,512]{2,1,0:T(8,128)(2,1)S(1)}, bf16[2,512,512]{2,1,0:T(8,128)(2,1)}, u32[]{:S(2)}) %copy-start.1) | copy-done | bytes 1048600
  4.6 0.0 copy-start.2
  4.6 1.2 %copy-done.2 = bf16[2,512,512]{2,1,0:T(8,128)(2,1)S(1)} copy-done((bf16[2,512,512]{2,1,0:T(8,128)(2,1)S(1)}, bf16[2,512,512]{2,1,0:T(8,128)(2,1)}, u32[]{:S(2)}) %copy-start.2) | copy-done | bytes 1048600
  5.8 0.0 copy-start.3
  5.8 1.0 %copy-done.3 = bf16[2,512,256]{2,1,0:T(8,128)(2,1)S(1)} copy-done((bf16[2,512,256]{2,1,0:T(8,128)(2,1)S(1)}, bf16[2,512,256]{2,1,0:T(8,128)(2,1)}, u32[]{:S(2)}) %copy-start.3) | copy-done | bytes 524312
  6.9 0.0 copy-start.4
  6.9 0.9 %copy-done.4 = bf16[2,512,128]{2,1,0:T(8,128)(2,1)S(1)} copy-done((bf16[2,512,128]{2,1,0:T(8,128)(2,1)S(1)}, bf16[2,512,128]{2,1,0:T(8,128)(2,1)}, u32[]{:S(2)}) %copy-start.4) | copy-done | bytes 262168
  7.8 0.0 copy-start.5
  7.8 0.7 %copy-done.5 = s32[32]{0:T(128)S(1)} copy-done((s32[32]{0:T(128)S(1)}, s32[32]{0:T(128)}, u32[]{:S(2)}) %copy-start.5) | copy-done | bytes 152
  8.5 55.0 %shard_map.100 = f32[2,512,512]{2,1,0:T(8,128)S(1)} custom-call(s32[32,4]{1,0:T(8,128)S(1)} %copy.11.partners, s32[32]{0:T(128)S(1)} %copy-done.5, bf16[2,512,512]{2,1,0:T(8,128)(2,1)S(1)} %copy-done, bf16[2,512,512]{2,1,0:T(8,128)(2,1)S(1)} %copy-done.1, bf16[2,512,512]{2,1,0:T(8,128)(2,1)S(1)} %copy-done.2, bf16[2,4,512,512]{3,2,1,0:T(8,128)(2,1)} %coupling.1, ...), custom_call_target="tpu_custom_call" | custom-call | tf_op jit(solution)/shard_map/pallas_call | solution.py:259
  63.5 1.3 %copy.15 = f32[2,512,512]{2,1,0:T(8,128)} copy(f32[2,512,512]{2,1,0:T(8,128)S(1)} %shard_map.100) | data formatting | bytes 4194304
Async XLA Ops:
  2.1 1.2 %copy-start = (bf16[2,512,512]{2,1,0:T(8,128)(2,1)S(1)}, bf16[2,512,512]{2,1,0:T(8,128)(2,1)}, u32[]{:S(2)}) copy-start(bf16[2,512,512]{2,1,0:T(8,128)(2,1)} %density.1) | copy-start | bytes 3145732
  3.4 1.2 %copy-start.1 = (bf16[2,512,512]{2,1,0:T(8,128)(2,1)S(1)}, bf16[2,512,512]{2,1,0:T(8,128)(2,1)}, u32[]{:S(2)}) copy-start(bf16[2,512,512]{2,1,0:T(8,128)(2,1)} %hcore.1) | copy-start | bytes 3145732
  4.6 1.2 %copy-start.2 = (bf16[2,512,512]{2,1,0:T(8,128)(2,1)S(1)}, bf16[2,512,512]{2,1,0:T(8,128)(2,1)}, u32[]{:S(2)}) copy-start(bf16[2,512,512]{2,1,0:T(8,128)(2,1)} %kernel.1) | copy-start | bytes 3145732
  5.8 1.0 %copy-start.3 = (bf16[2,512,256]{2,1,0:T(8,128)(2,1)S(1)}, bf16[2,512,256]{2,1,0:T(8,128)(2,1)}, u32[]{:S(2)}) copy-start(bf16[2,512,256]{2,1,0:T(8,128)(2,1)} %grid_basis.1) | copy-start | bytes 1572868
  6.9 0.9 %copy-start.4 = (bf16[2,512,128]{2,1,0:T(8,128)(2,1)S(1)}, bf16[2,512,128]{2,1,0:T(8,128)(2,1)}, u32[]{:S(2)}) copy-start(bf16[2,512,128]{2,1,0:T(8,128)(2,1)} %charge_map.1) | copy-start | bytes 786436
  7.8 0.7 %copy-start.5 = (s32[32]{0:T(128)S(1)}, s32[32]{0:T(128)}, u32[]{:S(2)}) copy-start(s32[32]{0:T(128)} %pair_count.1) | copy-start | bytes 388

commit v2 on v1

--- a/solution.py
+++ b/solution.py
@@ -22,10 +22,12 @@
 
 def fock_kernel(
     n, rows,
-    partners, pair_count, density, hcore, kernel, coupling, charge_map, charge_pos, grid_pos, grid_basis,
+    partners_in, counts_in, density, hcore, kernel, coupling, charge_map, charge_pos, grid_pos, grid_basis,
     fock,
     win, coup, resp, core, cmap, gbas, half, t_send, t_recv, t_own, dens_t, acc, pub, every, place,
+    relay, cpos, gpos, partners, pair_count,
     in_sem, out_sem, d_send_sem, d_recv_sem, t_send_sem, t_recv_sem, q_send_sem, q_recv_sem,
+    divert_sem, relay_sem, forward_sem,
 ):
     local, basis = density.shape[0], density.shape[1]
     slots = coupling.shape[1]
@@ -43,6 +45,10 @@
         pltpu.make_async_copy(kernel, resp, in_sem.at[3]),
         pltpu.make_async_copy(hcore, core, in_sem.at[4]),
         pltpu.make_async_copy(grid_basis, gbas, in_sem.at[5]),
+        pltpu.make_async_copy(charge_pos, cpos, in_sem.at[6]),
+        pltpu.make_async_copy(grid_pos, gpos, in_sem.at[7]),
+        pltpu.make_async_copy(partners_in, partners, in_sem.at[8]),
+        pltpu.make_async_copy(counts_in, pair_count, in_sem.at[9]),
     ]
     for load in loads:
         load.start()
@@ -81,14 +87,81 @@
 
     sends_to = (has_up, has_low)
     gets_from = (has_low, has_up)
-    for side in range(2):
-        @pl.when(sends_to[side])
-        def _():
-            for f in range(local):
+
+    place_in, layer = lax.rem(me, 4), lax.div(me, 4)
+
+    def diverted(side, i):
+        if n != 16 or local != 2 or i > 2:
+            return None
+        if side == 0:
+            return jnp.logical_and(place_in == 3, i < 3 - layer)
+        return jnp.logical_and(place_in == 0, i < layer)
+
+    def relays(side, i):
+        if n != 16 or local != 2 or i > 2:
+            return None
+        if side == 0:
+            return jnp.logical_and(place_in == 0, i < 3 - layer)
+        return jnp.logical_and(place_in == 3, i < layer)
+
+    def direct(side, i):
+        away = diverted(side, i)
+        if away is None:
+            return sends_to[side]
+        return jnp.logical_and(sends_to[side], jnp.logical_not(away))
+
+    def divert_copy(side, i, c):
+        part = pl.ds(c * rows, rows)
+        return pltpu.make_async_remote_copy(
+            src_ref=density.at[i, part] if i < local else t_send.at[side, i - local, part],
+            dst_ref=relay.at[i, part],
+            send_sem=divert_sem.at[i, c],
+            recv_sem=relay_sem.at[i, c],
+            device_id=(group, me - 3 if side == 0 else me + 3),
+            device_id_type=MESH,
+        )
+
+    def forward_copy(side, i, c):
+        part = pl.ds(c * rows, rows)
+        if i < local:
+            target = win.at[i if side == 0 else 2 * local + i, part]
+            arrived = d_recv_sem.at[side, i]
+        else:
+            target = t_recv.at[side, i - local, part]
+            arrived = t_recv_sem.at[side, i - local, c]
+        return pltpu.make_async_remote_copy(
+            src_ref=relay.at[i, part],
+            dst_ref=target,
+            send_sem=forward_sem.at[i, c],
+            recv_sem=arrived,
+            device_id=(group, me + 4 if side == 0 else me - 4),
+            device_id_type=MESH,
+        )
+
+    def pass_on(i):
+        for side in range(2):
+            if relays(side, i) is not None:
+                @pl.when(relays(side, i))
+                def _():
+                    for c in range(pieces):
+                        divert_copy(side, i, c).wait_recv()
+                        forward_copy(side, i, c).start()
+
+    for f in range(local):
+        for side in range(2):
+            if diverted(side, f) is not None:
+                @pl.when(diverted(side, f))
+                def _():
+                    for c in range(pieces):
+                        divert_copy(side, f, c).start()
+
+            @pl.when(direct(side, f))
+            def _():
                 dens_copy(side, f).start()
 
     loads[0].wait()
     loads[1].wait()
+    loads[6].wait()
     edge = 128
     eye = lax.broadcasted_iota(jnp.int32, (edge, edge), 0) == lax.broadcasted_iota(
         jnp.int32, (edge, edge), 1
@@ -101,7 +174,7 @@
             pops = jnp.sum(jnp.where(eye, block, 0.0), axis=1, keepdims=True)
             total = total + jnp.sum(pops * cmap[f, span, :].astype(F32), axis=0, keepdims=True)
         pub[f, 0:1, :] = total
-        pub[f, 1:4, :] = charge_pos[f]
+        pub[f, 1:4, :] = cpos[:, f, :]
     every[me] = pub[...]
 
     def publish(step):
@@ -122,12 +195,14 @@
     lax.fori_loop(1, n, publish_start, 0)
 
     loads[2].wait()
+    loads[8].wait()
+    loads[9].wait()
     live, position = [], []
     for f in range(local):
         count = pair_count[first + f]
         for k in range(slots):
             live.append(jnp.where(k < count, 1.0, 0.0).astype(F32))
-            position.append(partners[first + f, k] - (me - 1) * local)
+            position.append(partners[k, first + f] - (me - 1) * local)
     for f in range(local):
         for k in range(slots):
             half[f * slots + k] = (
@@ -156,14 +231,32 @@
                     t_send[0, w - 2 * local, span, cols] = value
         return carry
 
-    per_piece = rows // 32
-    for c in range(pieces):
-        lax.fori_loop(c * per_piece, (c + 1) * per_piece, gather_terms, 0)
+    lax.fori_loop(0, basis // 32, gather_terms, 0)
+
+    def send_terms(f):
         for side in range(2):
-            @pl.when(sends_to[side])
+            if diverted(side, local + f) is not None:
+                @pl.when(diverted(side, local + f))
+                def _():
+                    for c in range(pieces):
+                        divert_copy(side, local + f, c).start()
+
+            @pl.when(direct(side, local + f))
             def _():
-                for f in range(local):
+                for c in range(pieces):
                     term_copy(side, f, c).start()
+
+    pass_on(0)
+    late = relays(0, 1)
+    for f in range(local):
+        if late is None or f == 0:
+            send_terms(f)
+    if late is not None:
+        late = jnp.logical_or(late, relays(1, 1))
+
+        @pl.when(jnp.logical_not(late))
+        def _():
+            send_terms(1)
 
     loads[3].wait()
     loads[4].wait()
@@ -177,11 +270,17 @@
         publish(step).wait()
         return carry
 
+    pass_on(1)
+    if late is not None:
+        @pl.when(late)
+        def _():
+            send_terms(1)
     lax.fori_loop(1, n, publish_wait, 0)
     loads[5].wait()
+    loads[7].wait()
     for f in range(local):
         for axis in range(3):
-            place[axis] = jnp.broadcast_to(grid_pos[f, axis : axis + 1, :], (128, points)).T
+            place[axis] = jnp.broadcast_to(gpos[axis, f : f + 1, :], (128, points)).T
 
         field_parts = []
         strip = 64
@@ -207,6 +306,8 @@
         scaled = (gbas[f].astype(F32) * field).astype(BF16)
         acc[f] += dot_t(scaled, gbas[f])
 
+    pass_on(2)
+
     for side in range(2):
         @pl.when(gets_from[side])
         def _():
@@ -231,12 +332,25 @@
         pltpu.make_async_copy(acc.at[f], fock.at[f], out_sem.at[f]).start()
 
     for side in range(2):
-        @pl.when(sends_to[side])
-        def _():
-            for f in range(local):
-                dens_copy(side, f).wait_send()
-                for c in range(pieces):
-                    term_copy(side, f, c).wait_send()
+        for i in range(2 * local):
+            @pl.when(direct(side, i))
+            def _():
+                if i < local:
+                    dens_copy(side, i).wait_send()
+                else:
+                    for c in range(pieces):
+                        term_copy(side, i - local, c).wait_send()
+
+            if diverted(side, i) is not None:
+                @pl.when(diverted(side, i))
+                def _():
+                    for c in range(pieces):
+                        divert_copy(side, i, c).wait_send()
+
+                @pl.when(relays(side, i))
+                def _():
+                    for c in range(pieces):
+                        forward_copy(side, i, c).wait_send()
     for f in range(local):
         pltpu.make_async_copy(acc.at[f], fock.at[f], out_sem.at[f]).wait()
 
@@ -251,16 +365,14 @@
     charges = charge_map.shape[2]
     rows = 128
     pieces = basis // rows
-    anywhere = pl.BlockSpec(memory_space=pl.ANY)
-    smem = pl.BlockSpec(memory_space=pltpu.SMEM)
-    vmem = pl.BlockSpec(memory_space=pltpu.VMEM)
+    hbm = pl.BlockSpec(memory_space=pltpu.HBM)
     square = (basis, basis)
     dma = pltpu.SemaphoreType.DMA
     return pl.pallas_call(
         functools.partial(fock_kernel, n, rows),
         out_shape=jax.ShapeDtypeStruct((local,) + square, F32),
-        in_specs=[smem, smem, anywhere, anywhere, anywhere, anywhere, anywhere, vmem, vmem, anywhere],
-        out_specs=anywhere,
+        in_specs=[hbm] * 10,
+        out_specs=hbm,
         scratch_shapes=[
             pltpu.VMEM((3 * local,) + square, BF16),
             pltpu.VMEM((local, slots) + square, BF16),
@@ -277,7 +389,12 @@
             pltpu.VMEM((local, 4, charges), F32),
             pltpu.VMEM((n, local, 4, charges), F32),
             pltpu.VMEM((3, points, 128), F32),
-            dma((6,)),
+            pltpu.VMEM((3,) + square, BF16),
+            pltpu.VMEM((3, local, charges), F32),
+            pltpu.VMEM((3, local, points), F32),
+            pltpu.SMEM(partners.shape[::-1], jnp.int32),
+            pltpu.SMEM(pair_count.shape, jnp.int32),
+            dma((10,)),
             dma((local,)),
             dma((2, local)),
             dma((2, local)),
@@ -285,11 +402,15 @@
             dma((2, local, pieces)),
             dma((n,)),
             dma((n,)),
+            dma((3, pieces)),
+            dma((3, pieces)),
+            dma((3, pieces)),
         ],
         compiler_params=pltpu.CompilerParams(
-            collective_id=0, has_side_effects=True, vmem_limit_bytes=48 * 1024 * 1024
+            collective_id=0, has_side_effects=True, vmem_limit_bytes=63 * 1024 * 1024
         ),
-    )(partners, pair_count, density, hcore, kernel, coupling, charge_map, charge_pos, grid_pos, grid_basis)
+    )(partners.T, pair_count, density, hcore, kernel, coupling, charge_map,
+      jnp.swapaxes(charge_pos, 0, 1), jnp.swapaxes(grid_pos, 0, 1), grid_basis)
 
 
 def solution(mesh):

time: 65.5 us -> 52.9 us (0.81)
  local copies, waits for them, and re-layouts: 9.78 us -> 3.08 us
  Pallas kernels: 55 us -> 49.6 us
    unnamed x16 -> x1, local copies, waits for them, and re-layouts: 9.78 us -> 3.08 us
    pallas_call x1, Pallas kernels: 55 us -> 49.6 us  [body(): pl.pallas_call(functools.partial(fock_kernel, n, rows), out_shape=jax.Sha...]
where the time goes in v2:
time: 52.9 us; the launch traced here: 52.7 us
  Pallas kernels  49.6 us (94%)
  local copies, waits for them, and re-layouts  3.08 us (6%)
    pallas_call x1, Pallas kernels, body(): pl.pallas_call(functools.partial(fock_kernel, n, rows), out_shape=jax.Sha...  49.6 us
    unnamed x1, local copies, waits for them, and re-layouts  3.08 us

profile of v2, /device:TPU:1, one launch (start us, length us, event | category | flops | bytes accessed | tf_op | source)
XLA Modules:
  0.0 52.7 jit_solution(12147053780441357527)
XLA Ops:
  0.0 49.6 %shard_map.100 = f32[2,512,512]{2,1,0:T(8,128)} custom-call(s32[4,32]{1,0:T(4,128)} %bitcast.5, s32[32]{0:T(128)} %counts_in.1, bf16[2,512,512]{2,1,0:T(8,128)(2,1)} %density.1, bf16[2,512,512]{2,1,0:T(8,128)(2,1)} %hcore.1, bf16[2,512,512]{2,1,0:T(8,128)(2,1)} %kernel.1, bf16[2,4,512,512]{3,2,1,0:T(8,128)(2,1)} %coupling.1, ...), custom_call_target="tpu_custom_call" | custom-call | tf_op jit(solution)/shard_map/pallas_call | solution.py:371
  49.6 3.1 %copy.12 = f32[2,512,512]{2,1,0:T(8,128)} copy(f32[2,512,512]{2,1,0:T(8,128)} %shard_map.100) | data formatting | bytes 4194304

commit v3 on v2

--- a/solution.py
+++ b/solution.py
@@ -318,6 +318,10 @@
             where = jnp.clip(position[f * slots + k], 0, 3 * local - 1)
             acc[f] += dot(half[f * slots + k], win[where])
 
+    def result_copy(f, c):
+        part = pl.ds(pl.multiple_of(c * rows, rows), rows)
+        return pltpu.make_async_copy(acc.at[f, :, part], fock.at[f, :, part], out_sem.at[f, c])
+
     for f in range(local):
         def add_piece(c, carry):
             part = pl.ds(pl.multiple_of(c * rows, rows), rows)
@@ -326,10 +330,10 @@
                 def _():
                     term_copy(side, f, c).wait_recv()
                     acc[f, :, part] += dot_t(dens_t[f], t_recv[side, f, part, :])
+            result_copy(f, c).start()
             return carry
 
         lax.fori_loop(0, pieces, add_piece, 0)
-        pltpu.make_async_copy(acc.at[f], fock.at[f], out_sem.at[f]).start()
 
     for side in range(2):
         for i in range(2 * local):
@@ -352,7 +356,8 @@
                     for c in range(pieces):
                         forward_copy(side, i, c).wait_send()
     for f in range(local):
-        pltpu.make_async_copy(acc.at[f], fock.at[f], out_sem.at[f]).wait()
+        for c in range(pieces):
+            result_copy(f, c).wait()
 
 
 def body(
@@ -395,7 +400,7 @@
             pltpu.SMEM(partners.shape[::-1], jnp.int32),
             pltpu.SMEM(pair_count.shape, jnp.int32),
             dma((10,)),
-            dma((local,)),
+            dma((local, pieces)),
             dma((2, local)),
             dma((2, local)),
             dma((2, local, pieces)),

time: 52.9 us -> 52.6 us (level)
  no operation moved by 1% of the time
where the time goes in v3:
time: 52.6 us; the launch traced here: 52.5 us
  Pallas kernels  49.4 us (94%)
  local copies, waits for them, and re-layouts  3.08 us (6%)
    pallas_call x1, Pallas kernels, body(): pl.pallas_call(functools.partial(fock_kernel, n, rows), out_shape=jax.Sha...  49.4 us
    unnamed x1, local copies, waits for them, and re-layouts  3.08 us

profile of v3, /device:TPU:1, one launch (start us, length us, event | category | flops | bytes accessed | tf_op | source)
XLA Modules:
  0.0 52.5 jit_solution(15647030139951042825)
XLA Ops:
  0.0 49.4 %shard_map.100 = f32[2,512,512]{2,1,0:T(8,128)} custom-call(s32[4,32]{1,0:T(4,128)} %bitcast.5, s32[32]{0:T(128)} %counts_in.1, bf16[2,512,512]{2,1,0:T(8,128)(2,1)} %density.1, bf16[2,512,512]{2,1,0:T(8,128)(2,1)} %hcore.1, bf16[2,512,512]{2,1,0:T(8,128)(2,1)} %kernel.1, bf16[2,4,512,512]{3,2,1,0:T(8,128)(2,1)} %coupling.1, ...), custom_call_target="tpu_custom_call" | custom-call | tf_op jit(solution)/shard_map/pallas_call | solution.py:376
  49.4 3.1 %copy.12 = f32[2,512,512]{2,1,0:T(8,128)} copy(f32[2,512,512]{2,1,0:T(8,128)} %shard_map.100) | data formatting | bytes 4194304
